TPU v7x, 512 devices: a whole 4x4x16 slice. The times are simulated.
512 devices in a mesh: dp: 4 (over x), tensor: 8 (over y, core), pipe: 16 (over z).
Axes of the slice: x: 4, y: 4, z: 16, core: 2. Of those that a mesh axis runs over, the one named last changes fastest.
Arguments:
- tokens: bfloat16 [1024, 4096], P(('dp', 'pipe'), 'tensor'), parts along dimension 0, may hold values from -6 to 6
- final_gain: float32 [4096], replicated, may hold values from 0.5 to 1.5
- unembed: bfloat16 [76800, 4096], P(('tensor', 'pipe')), may hold values from -0.28125 to 0.28125
- targets: int32 [1024], P('dp'), parts along dimension 0, may hold values from 0 to 76799
Outputs:
- row_loss: float32 [1024], P('dp'), parts along dimension 0
- tokens_grad: float32 [1024, 4096], P(('dp', 'pipe'), 'tensor'), parts along dimension 0
There are 4 independent parts, one for each index of `dp`. A program takes and returns all parts, laid end to end along the dimension named above; an argument that names none is the same for every part. Nothing has to cross between parts.
All inputs are finite; a program needn't handle non-finite values.
Results may differ from a plain program's by a relative error of at most 0.0045.
Values may be sent and summed in bfloat16 or wider, within the bound.
A program may use at most 64 MiB of HBM per device.

v0:
```python
import jax
import jax.numpy as jnp
from jax import lax
from jax.sharding import PartitionSpec as P

EPS = 1e-06


def body(tokens, final_gain, unembed, targets):
    width_all = final_gain.shape[0]
    column_width = tokens.shape[1]
    tensor_count = lax.axis_size("tensor")
    stream = tokens.astype(jnp.float32)
    squares = lax.psum(jnp.sum(stream * stream, axis=1), "tensor")
    inv_rms = lax.rsqrt(squares / width_all + EPS)
    column_start = lax.axis_index("tensor") * column_width
    gain_part = lax.dynamic_slice_in_dim(final_gain, column_start, column_width)
    scaled = (stream * inv_rms[:, None] * gain_part[None, :]).astype(jnp.bfloat16)
    final = lax.all_gather(scaled, "tensor", axis=1, tiled=True)
    dims = (((1,), (1,)), ((), ()))
    all_rows = lax.all_gather(final, "pipe", axis=0, tiled=True)
    logits_t = lax.dot_general(unembed, all_rows, dims, preferred_element_type=jnp.float32)
    vocab_local = unembed.shape[0]
    all_positions = logits_t.shape[1]
    vocab_start = lax.axis_index(("tensor", "pipe")) * vocab_local
    local_ids = targets - vocab_start
    vocab_mask = (jnp.arange(vocab_local, dtype=jnp.int32)[:, None] == local_ids[None, :]).astype(
        jnp.float32
    )
    picked_local = jnp.sum(vocab_mask * logits_t, axis=0)
    local_top = jnp.max(logits_t, axis=0)
    row_top = lax.pmax(local_top, ("tensor", "pipe"))
    exp_local = jnp.sum(jnp.exp(logits_t - row_top[None, :]), axis=0)
    exp_total, picked = lax.psum((exp_local, picked_local), ("tensor", "pipe"))
    log_total = row_top + jnp.log(exp_total)
    row_loss = log_total - picked
    probs_diff = (jnp.exp(logits_t - log_total[None, :]) - vocab_mask).astype(jnp.bfloat16)
    unembed_split = unembed.reshape(vocab_local, tensor_count, column_width)
    term = jnp.einsum("vr,vtd->trd", probs_diff, unembed_split, preferred_element_type=jnp.float32)
    term = term.reshape(tensor_count * all_positions, column_width)
    final_grad = lax.psum_scatter(term, ("tensor", "pipe"), scatter_dimension=0, tiled=True)
    weighted = final_grad * gain_part[None, :]
    dots = lax.psum(jnp.sum(weighted * stream, axis=1), "tensor") / width_all
    tokens_grad = inv_rms[:, None] * (weighted - stream * (inv_rms * inv_rms * dots)[:, None])
    return (row_loss, tokens_grad)


def solution(mesh):
    placed = (P(("dp", "pipe"), "tensor"), P(), P(("tensor", "pipe"), None), P("dp"))
    return jax.shard_map(
        body,
        mesh=mesh,
        in_specs=placed,
        out_specs=(P("dp"), P(("dp", "pipe"), "tensor")),
        check_vma=False,
    )
```

profile of v0, /device:TPU:1, one launch (start us, length us, event | category | flops | bytes accessed | tf_op | source)
XLA Modules:
  0.0 898.9 jit_solution(970221941042293635)
XLA Ops:
  7.2 0.0 all-gather.2.cloned.1.call-start
  7.2 0.8 fusion.13
  8.0 18.6 %psum.28 = f32[16]{0:T(128)S(1)} all-reduce(f32[16]{0:T(128)S(1)} %fusion.13), channel_id=1, replica_groups=mesh['dp'=4,'tensor'=8,'pipe'=16] {'tensor'}, use_global_device_ids=true, to_apply=%region_1.0 | all-reduce | flops 16 | bytes 128 | tf_op jit(solution)/shard_map/psum | solution.py:14
  26.7 0.8 dynamic_slice.3
  27.5 0.8 fusion.15
  28.3 14.4 %all_gather.6 = bf16[16,4096]{1,0:T(8,128)(2,1)} all-gather(bf16[16,512]{1,0:T(8,128)(2,1)S(1)} %fusion.15), channel_id=1, replica_groups=mesh['dp'=4,'tensor'=8,'pipe'=16] {'tensor'}, dimensions={1}, use_global_device_ids=true | all-gather | bytes 147456 | tf_op jit(solution)/shard_map/all_gather | solution.py:19
  42.7 0.0 all-gather.2.cloned.1.call-update
  42.7 0.0 reduce-scatter.2.cloned.1.call-start
  42.7 0.7 broadcast_subtract_fusion
  43.4 62.8 %all-gather.2.cloned.1.call-done = bf16[256,4096]{1,0:T(8,128)(2,1)} async-done(((bf16[16,4096]{1,0:T(8,128)(2,1)}), bf16[256,4096]{1,0:T(8,128)(2,1)}) %all-gather.2.cloned.1.call-update) | async-done | bytes 2097168 | tf_op jit(solution)/shard_map/all_gather | solution.py:21
  106.2 4.5 fusion.20
  110.7 240.3 %pmax.7 = f32[256]{0:T(256)S(1)} all-reduce(f32[256]{0:T(256)S(1)} %get-tuple-element.8), channel_id=1, replica_groups=mesh['dp'=4,'tensor'=8,'pipe'=16] {'tensor','pipe'}, use_global_device_ids=true, to_apply=%region_3.0 | all-reduce | flops 256 | bytes 2048 | tf_op jit(solution)/shard_map/pmax | solution.py:32
  351.0 0.2 fusion.5
  351.2 247.7 %all-reduce = (f32[256]{0:T(256)S(1)}, f32[256]{0:T(256)S(1)}) all-reduce(f32[256]{0:T(256)S(1)} %get-tuple-element.3, f32[256]{0:T(256)S(1)} %get-tuple-element.2), channel_id=1, replica_groups=mesh['dp'=4,'tensor'=8,'pipe'=16] {'tensor','pipe'}, use_global_device_ids=true, to_apply=%region_5.0 | all-reduce | flops 512 | bytes 4096 | tf_op jit(solution)/shard_map/psum | solution.py:34
  598.9 0.6 fusion.19
  599.5 0.0 copy-start
  599.5 6.2 fusion
  605.8 0.0 reduce-scatter.2.cloned.1.call-update
  605.8 260.3 %reduce-scatter.2.cloned.1.call-done = f32[16,512]{1,0:T(8,128)} async-done(((f32[2048,512]{1,0:T(8,128)}), f32[16,512]{1,0:T(8,128)}) %reduce-scatter.2.cloned.1.call-update) | async-done | bytes 32784 | tf_op jit(solution)/shard_map/reduce_scatter | solution.py:41
  866.1 0.0 copy-done
  866.1 0.9 fusion.16
  866.9 23.6 %psum.31 = f32[16]{0:T(128)S(1)} all-reduce(f32[16]{0:T(128)S(1)} %fusion.16), channel_id=1, replica_groups=mesh['dp'=4,'tensor'=8,'pipe'=16] {'tensor'}, use_global_device_ids=true, to_apply=%region_10.0 | all-reduce | flops 16 | bytes 128 | tf_op jit(solution)/shard_map/psum | solution.py:43
  890.6 1.5 fusion.18
  (2 shorter events, 0.0 us)
Async XLA Ops:
  7.2 99.0 %all-gather.2.cloned.1.call-start = ((), (), s32[]{:S(2)}) async-start(), calls=%async_computation.1 | async-start | bytes 2228224 | tf_op jit(solution)/shard_map/all_gather | solution.py:21
  42.7 823.4 %reduce-scatter.2.cloned.1.call-start = ((), (), s32[]{:S(2)}) async-start(), calls=%async_computation.2 | async-start | bytes 4227072 | tf_op jit(solution)/shard_map/reduce_scatter | solution.py:41
  599.5 266.5 %copy-start = (bf16[16,512]{1,0:T(8,128)(2,1)S(1)}, bf16[16,512]{1,0:T(8,128)(2,1)}, u32[]{:S(2)}) copy-start(bf16[16,512]{1,0:T(8,128)(2,1)} %param.4) | copy-start | bytes 49156
Sparse Core Ops, SparseCore 0:
  42.8 63.3 all-gather.1
  605.9 260.1 reduce-scatter.1
where the time goes:
time: 899 us
  blocking collectives  545 us (61%)
  waiting for transfers between devices  323 us (36%)
  between operations  14.1 us (2%)
  matrix products  10.8 us (1%)
    reduce_scatter x1, waiting for transfers between devices, body(): lax.psum_scatter(term, ('tensor', 'pipe'), scatter_dimension=0, tiled=True)  260 us
    psum x1, blocking collectives, body(): exp_total, picked = lax.psum((exp_local, picked_local), ('tensor', 'pipe'))  248 us
    pmax x1, blocking collectives, body(): row_top = lax.pmax(local_top, ('tensor', 'pipe'))  240 us
    all_gather x1, waiting for transfers between devices, body(): all_rows = lax.all_gather(final, 'pipe', axis=0, tiled=True)  62.8 us
    psum x1, blocking collectives, body(): dots = lax.psum(jnp.sum(weighted * stream, axis=1), 'tensor') / width_all  23.6 us
    psum x1, blocking collectives, body(): squares = lax.psum(jnp.sum(stream * stream, axis=1), 'tensor')  18.6 us
  transfers between devices with their start and end apart: 2, of which 2 were waited for; matrix products, arithmetic and copies ran while one was open for 0% of the time, Pallas kernels for 0%

commit v1 on v0

v1 whole, which is shorter than its diff:
```python
import functools

import jax
import jax.numpy as jnp
from jax import lax
from jax.experimental import pallas as pl
from jax.experimental.pallas import tpu as pltpu
from jax.sharding import PartitionSpec as P

EPS = 1e-06
MESH = pl.DeviceIdType.MESH
NY, NC, NZ = 4, 2, 16
NT = NY * NC
BLK = 16
F32, BF16 = jnp.float32, jnp.bfloat16
GROUPS = [[(0, 1)], [(1, 2), (14, 2)], [(3, 2), (12, 2)], [(5, 7)]]
Z_ORDER = [8, 7, 9, 6, 10, 5, 11, 4, 12, 3, 13, 2, 14, 1, 15]
Y_ORDER = [2, 1, 3]


def kernel(
    tok_ref, gain_ref, tgt_ref, u_hbm, loss_ref, grad_ref,
    xs, us, ug, logits, q, term, send_t, send_o, core_t, core_o, y_t, y_o, own, z_send, z_recv,
    stat_send, stat_y, group, stat_z, twice, twice_int, u_sem, send_sem, recv_sem,
):
    dp = lax.axis_index("dp")
    t = lax.axis_index("tensor")
    z = lax.axis_index("pipe")
    y, c = t // NC, t % NC
    rows = BLK * NZ
    width = tok_ref.shape[1]
    vocab = us.shape[1]
    count = [0]
    started = []

    def tensor_of(dy, dc):
        return lax.rem(y + dy, NY) * NC + lax.rem(c + dc, NC)

    def at_tensor(dy, dc):
        return (dp, tensor_of(dy, dc), z)

    def at_pipe(d):
        return (dp, t, lax.rem(z + d, NZ))

    def send(src, dst, device):
        i = count[0]
        count[0] += 1
        copy = pltpu.make_async_remote_copy(
            src_ref=src, dst_ref=dst, send_sem=send_sem.at[i], recv_sem=recv_sem.at[i],
            device_id=device, device_id_type=MESH,
        )
        copy.start()
        started.append(copy)
        return copy

    barrier = pltpu.get_barrier_semaphore()
    for d in range(1, NZ):
        pl.semaphore_signal(barrier, inc=1, device_id=at_pipe(d), device_id_type=MESH)
    for j in range(1, NT):
        pl.semaphore_signal(barrier, inc=1, device_id=at_tensor(j // NC, j % NC), device_id_type=MESH)

    loads = []
    for k in range(NT):
        load = pltpu.make_async_copy(u_hbm.at[:, pl.ds(k * width, width)], us.at[k], u_sem.at[k])
        load.start()
        loads.append(load)
    own_copy = pltpu.make_async_copy(tok_ref, xs.at[t, pl.ds(0, BLK)], u_sem.at[NT])
    own_copy.start()

    for h in range(2):
        part = jnp.transpose(jnp.broadcast_to(tgt_ref[h : h + 1, :], (128, 128)))
        twice_int[pl.ds(h * 128, 128), :] = part
        twice_int[pl.ds(rows + h * 128, 128), :] = part
    shift = pl.multiple_of(z * BLK, BLK)
    back = pl.multiple_of(rows - z * BLK, BLK)
    vocab_start = (t * NZ + z) * vocab
    own_copy.wait()

    pl.semaphore_wait(barrier, NZ - 1 + NT - 1)

    z_copies = {}
    for d in Z_ORDER:
        z_copies[d] = send(tok_ref, xs.at[t, pl.ds((NZ - d) * BLK, BLK)], at_pipe(d))
    y_copies, core_own = [], []

    def forward(g):
        for first, number in GROUPS[g]:
            piece = xs.at[t, pl.ds(first * BLK, number * BLK)]
            for dy in Y_ORDER:
                y_copies.append((g, dy, first, number, send(piece, piece, at_tensor(dy, 0))))
            core_own.append(send(piece, piece, at_tensor(0, 1)))

    core_far = []

    def hand_over(g):
        for group_of, dy, first, number, copy in y_copies:
            if group_of == g:
                copy.wait_recv()
                source = tensor_of(NY - dy, 0)
                piece = xs.at[source, pl.ds(first * BLK, number * BLK)]
                core_far.append(send(piece, piece, at_tensor(0, 1)))

    def wait_group(g):
        for first, number in GROUPS[g]:
            for s in range(first, first + number):
                z_copies[NZ - s].wait_recv()

    forward(0)
    for k in range(NT):
        loads[k].wait()

    def scale_u(k, _):
        ug[k] = (us[k].astype(F32) * gain_ref[pl.ds(k, 1), :]).astype(BF16)
        return 0

    lax.fori_loop(0, NT, scale_u, 0)
    wait_group(1)
    forward(1)
    hand_over(0)

    lane = lax.broadcasted_iota(jnp.int32, (rows, vocab), 1)
    local = twice_int[pl.ds(shift, rows), :] - vocab_start
    local5 = jnp.concatenate([local] * 5, axis=1)[:, :vocab]
    onehot = (lane == local5).astype(F32).astype(BF16)
    q[...] = onehot

    def pick_row(k, _):
        send_o[k] = jnp.dot(q[...], us[k], preferred_element_type=F32).astype(BF16)
        return 0

    lax.fori_loop(0, NT, pick_row, 0)
    wait_group(2)
    forward(2)
    hand_over(1)
    wait_group(3)
    forward(3)
    o_core = []
    for dy in range(NY):
        o_core.append(send(send_o.at[tensor_of(dy, 1)], core_o.at[dy], at_tensor(0, 1)))
    hand_over(2)
    o_y = {}
    for dy in Y_ORDER + [0]:
        o_core[dy].wait_recv()
        mine = tensor_of(dy, 0)
        send_o[mine] = (send_o[mine].astype(F32) + core_o[dy].astype(F32)).astype(BF16)
        if dy:
            o_y[dy] = send(send_o.at[mine], y_o.at[dy - 1], at_tensor(dy, 0))
    hand_over(3)
    for copy in core_own + core_far:
        copy.wait_recv()

    logits[...] = jnp.zeros_like(logits)

    def multiply(k, total):
        x = xs[k]
        logits[...] += lax.dot_general(x, ug[k], (((1,), (1,)), ((), ())), preferred_element_type=F32)
        xf = x.astype(F32)
        xf = xf * xf
        for i in range(width // 128):
            total = total + xf[:, i * 128 : (i + 1) * 128]
        return total

    squares = lax.fori_loop(0, NT, multiply, jnp.zeros((rows, 128), F32))
    inv = lax.rsqrt(jnp.sum(squares, axis=1, keepdims=True) / (width * NT) + EPS)
    own_inv = inv[:BLK]
    twice[pl.ds(0, rows), :] = jnp.broadcast_to(inv, (rows, 128))
    lane_id = lax.broadcasted_iota(jnp.int32, (64, 128), 1)
    column = lax.broadcasted_iota(jnp.int32, (64, vocab), 1)
    for r in range(0, rows, 64):
        part = pl.ds(r, 64)
        l = logits[part, :] * twice[part, :][:, :1]
        tgt = twice_int[pl.ds(pl.multiple_of(shift + r, BLK), 64), :][:, :1] - vocab_start
        here = column == tgt
        top = jnp.max(l, axis=1, keepdims=True)
        e = jnp.where(here, 0.0, jnp.exp(l - top))
        q[part, :] = e.astype(BF16)
        total = jnp.sum(e, axis=1, keepdims=True)
        mixed = jnp.sum(e * l, axis=1, keepdims=True)
        picked = jnp.sum(jnp.where(here, l, 0.0), axis=1, keepdims=True)
        stats = jnp.where(lane_id == 0, top, jnp.where(lane_id == 1, total, jnp.where(lane_id == 2, mixed, picked)))
        twice[part, :] = stats
        twice[pl.ds(rows + r, 64), :] = stats
    for h in range(2):
        across = jnp.transpose(twice[pl.ds(pl.multiple_of(back + h * 128, BLK), 128), :]) if h == 0 else jnp.transpose(
            twice[pl.ds(pl.multiple_of(lax.rem(back + h * 128, rows), BLK), 128), :])
        for i in range(4):
            stat_send[pl.ds(2 * i + h, 1), :] = across[i : i + 1, :]
    y_stats = []
    for j in range(1, NT):
        y_stats.append(send(stat_send, stat_y.at[j], at_tensor(j // NC, j % NC)))

    def gradient(k, _):
        term[k] = jnp.dot(q[...], us[k], preferred_element_type=F32)
        return 0

    lax.fori_loop(0, NT, gradient, 0)

    def merge(tiles):
        top = tiles[0][0:2]
        for tile in tiles[1:]:
            top = jnp.maximum(top, tile[0:2])
        total = mixed = picked = jnp.zeros((2, 128), F32)
        for tile in tiles:
            factor = jnp.exp(tile[0:2] - top)
            total = total + factor * tile[2:4]
            mixed = mixed + factor * tile[4:6]
            picked = picked + tile[6:8]
        return top, total, mixed, picked

    def spread(value):
        for h in range(2):
            part = jnp.transpose(jnp.broadcast_to(value[h : h + 1, :], (128, 128)))
            twice[pl.ds(h * 128, 128), :] = part
            twice[pl.ds(rows + h * 128, 128), :] = part
        return twice[pl.ds(shift, rows), :]

    for copy in y_stats:
        copy.wait_recv()
    mine = stat_send[...]
    top, total, mixed, picked = merge([mine] + [stat_y[j] for j in range(1, NT)])
    group[0:2, :] = top
    group[2:4, :] = total
    group[4:6, :] = mixed
    group[6:8, :] = picked
    z_stats = []
    for d in Z_ORDER:
        z_stats.append(send(group, stat_z.at[d], at_pipe(d)))
    factor = spread(jnp.exp(mine[0:2] - top))
    factor4 = jnp.concatenate([factor] * (width // 128), axis=1)

    def rounded(k, _):
        send_t[k] = (term[k] * factor4).astype(BF16)
        return 0

    lax.fori_loop(0, NT, rounded, 0)
    t_core = {}
    for dy in Y_ORDER + [0]:
        t_core[dy] = send(send_t.at[tensor_of(dy, 1)], core_t.at[dy], at_tensor(0, 1))
    t_y = {}
    far, near = [(4, 8)], [(12, 4), (0, 4)]
    for dy in Y_ORDER:
        t_core[dy].wait_recv()
        k = tensor_of(dy, 0)
        send_t[k] = (send_t[k].astype(F32) + core_t[dy].astype(F32)).astype(BF16)
        for first, number in far + near:
            piece = pl.ds(first * BLK, number * BLK)
            t_y[dy, first] = send(send_t.at[k, piece], y_t.at[dy - 1, piece], at_tensor(dy, 0))
    t_core[0].wait_recv()
    for dy in Y_ORDER:
        o_y[dy].wait_recv()
    for copy in z_stats:
        copy.wait_recv()
    group_top = group[0:2]
    top, total, mixed, picked = merge([group[...]] + [stat_z[d] for d in range(1, NZ)])
    at_target = jnp.exp(picked - top)
    full = total + at_target
    loss_ref[...] = top + jnp.log(full) - picked
    kept = total / full
    scale = spread(jnp.exp(group_top - top) / full)
    own[...] = scale
    drop = spread(kept)
    own_dot = spread((mixed - total * picked) / full)[:BLK]
    z_grads = {}
    for part_of in (far, near):
        for first, number in part_of:
            piece = pl.ds(first * BLK, number * BLK)
            for dy in Y_ORDER:
                t_y[dy, first].wait_recv()
            value = send_t[t, piece, :].astype(F32) + core_t[0, piece, :].astype(F32)
            target = send_o[t, piece, :].astype(F32)
            for dy in range(NY - 1):
                value = value + y_t[dy, piece, :].astype(F32)
                target = target + y_o[dy, piece, :].astype(F32)
            a = own[piece, :]
            b = drop[first * BLK : (first + number) * BLK]
            for i in range(width // 128):
                cut = slice(i * 128, (i + 1) * 128)
                v = value[:, cut] * a - target[:, cut] * b
                z_send[piece, cut] = v.astype(BF16)
                if first == 0:
                    term[0, pl.ds(0, BLK), cut] = v[:BLK]
        for d in Z_ORDER:
            if any(first <= d < first + number for first, number in part_of):
                z_grads[d] = send(z_send.at[pl.ds(d * BLK, BLK)], z_recv.at[d], at_pipe(d))
    grad = term[0, pl.ds(0, BLK), :]
    for d in reversed(Z_ORDER):
        z_grads[d].wait_recv()
        grad = grad + z_recv[d].astype(F32)
    stream = tok_ref[...].astype(F32)
    weighted = grad * gain_ref[pl.ds(t, 1), :]
    dots = own_dot[:, :1] / (own_inv * (width * NT))
    grad_ref[...] = own_inv * (weighted - stream * (own_inv * own_inv * dots))
    for copy in started:
        copy.wait_send()


def body(tokens, final_gain, unembed, targets):
    vocab, features = unembed.shape
    width = tokens.shape[1]
    rows = targets.shape[0]
    vmem = pl.BlockSpec(memory_space=pltpu.VMEM)
    loss, grad = pl.pallas_call(
        kernel,
        out_shape=(
            jax.ShapeDtypeStruct((2, 128), F32),
            jax.ShapeDtypeStruct(tokens.shape, F32),
        ),
        in_specs=[vmem, vmem, vmem, pl.BlockSpec(memory_space=pl.ANY)],
        out_specs=(vmem, vmem),
        scratch_shapes=[
            pltpu.VMEM((NT, rows, width), BF16),
            pltpu.VMEM((NT, vocab, width), BF16),
            pltpu.VMEM((NT, vocab, width), BF16),
            pltpu.VMEM((rows, vocab), F32),
            pltpu.VMEM((rows, vocab), BF16),
            pltpu.VMEM((NT, rows, width), F32),
            pltpu.VMEM((NT, rows, width), BF16),
            pltpu.VMEM((NT, rows, width), BF16),
            pltpu.VMEM((NY, rows, width), BF16),
            pltpu.VMEM((NY, rows, width), BF16),
            pltpu.VMEM((NY - 1, rows, width), BF16),
            pltpu.VMEM((NY - 1, rows, width), BF16),
            pltpu.VMEM((rows, 128), F32),
            pltpu.VMEM((rows, width), BF16),
            pltpu.VMEM((NZ, BLK, width), BF16),
            pltpu.VMEM((8, 128), F32),
            pltpu.VMEM((NT, 8, 128), F32),
            pltpu.VMEM((8, 128), F32),
            pltpu.VMEM((NZ, 8, 128), F32),
            pltpu.VMEM((2 * rows, 128), F32),
            pltpu.VMEM((2 * rows, 128), jnp.int32),
            pltpu.SemaphoreType.DMA((NT + 1,)),
            pltpu.SemaphoreType.DMA((160,)),
            pltpu.SemaphoreType.DMA((160,)),
        ],
        compiler_params=pltpu.CompilerParams(
            collective_id=0, has_side_effects=True, vmem_limit_bytes=60 * 1024 * 1024
        ),
    )(tokens, final_gain.reshape(NT, width), targets.reshape(2, 128), unembed)
    return loss.reshape(rows), grad


def solution(mesh):
    placed = (P(("dp", "pipe"), "tensor"), P(), P(("tensor", "pipe"), None), P("dp"))
    return jax.shard_map(
        body,
        mesh=mesh,
        in_specs=placed,
        out_specs=(P("dp"), P(("dp", "pipe"), "tensor")),
        check_vma=False,
    )
```

time: 899 us -> 92.1 us (0.10)
  blocking collectives: 545 us -> 0 us
  waiting for transfers between devices: 323 us -> 0 us
  Pallas kernels: 0 us -> 87.2 us
  between operations: 14.1 us -> 0.64 us
  matrix products: 10.8 us -> 0 us
    psum x3 -> x0, blocking collectives: 290 us -> none  [the longest x1 248 us: body(): exp_total, picked = lax.psum((exp_local, picked_local), ('tensor', 'pipe'))]
    reduce_scatter x1 -> x0, waiting for transfers between devices: 260 us -> none  [body(): lax.psum_scatter(term, ('tensor', 'pipe'), scatter_dimension=0, tiled=True)]
    pmax x1 -> x0, blocking collectives: 240 us -> none  [body(): row_top = lax.pmax(local_top, ('tensor', 'pipe'))]
    pallas_call x0 -> x1, Pallas kernels: none -> 87.2 us  [body(): pl.pallas_call(kernel, out_shape=(jax.ShapeDtypeStruct((2, 128), F32), ja...]
    all_gather x1 -> x0, waiting for transfers between devices: 62.8 us -> none  [body(): all_rows = lax.all_gather(final, 'pipe', axis=0, tiled=True)]
    all_gather x1 -> x0, blocking collectives: 14.4 us -> none  [body(): final = lax.all_gather(scaled, 'tensor', axis=1, tiled=True)]
    dot_general x2 -> x0, matrix products: 10.8 us -> none  [the longest x1 6.24 us: body(): jnp.einsum('vr,vtd->trd', probs_diff, unembed_split, preferred_element_ty...]
  transfers between devices with their start and end apart: 2 -> 0, of which waited for: 2 -> 0; matrix products, arithmetic and copies ran while one was open for 0% -> 0% of each run, Pallas kernels for 0% -> 0%
where the time goes in v1:
time: 92.1 us; the launch traced here: 91.8 us
  Pallas kernels  87.2 us (95%)
  local copies, waits for them, and re-layouts  3.93 us (4%)
    pallas_call x1, Pallas kernels, body(): pl.pallas_call(kernel, out_shape=(jax.ShapeDtypeStruct((2, 128), F32), ja...  87.2 us
    unnamed x2, local copies, waits for them, and re-layouts  2.6 us

profile of v1, /device:TPU:1, one launch (start us, length us, event | category | flops | bytes accessed | tf_op | source)
XLA Modules:
  0.0 91.8 jit_solution(12117778156034999179)
XLA Ops:
  0.6 1.3 %reshape.13.gain_ref = f32[8,512]{1,0:T(8,128)} reshape(f32[4096]{0:T(1024)} %param.5) | data formatting | bytes 32768 | tf_op jit(solution)/shard_map/reshape | solution.py:339
  2.0 87.2 %shard_map.59 = (f32[2,128]{1,0:T(2,128)}, f32[16,512]{1,0:T(8,128)}) custom-call(bf16[16,512]{1,0:T(8,128)(2,1)} %tok_ref.1, f32[8,512]{1,0:T(8,128)} %reshape.13.gain_ref, s32[2,128]{1,0:T(2,128)} %bitcast.3, bf16[600,4096]{1,0:T(8,128)(2,1)} %u_hbm.1), custom_call_target="tpu_custom_call" | custom-call | tf_op jit(solution)/shard_map/pallas_call | solution.py:302
  89.2 1.2 %copy.8 = f32[256]{0:T(256)} copy(f32[256]{0:T(256)} %bitcast.2) | data formatting | bytes 2048
  90.4 1.4 %copy.9 = f32[16,512]{1,0:T(8,128)} copy(f32[16,512]{1,0:T(8,128)} %get-tuple-element.9) | data formatting | bytes 65536

commit v2 on v1

v2 whole, which is shorter than its diff:
```python
import functools

import jax
import jax.numpy as jnp
from jax import lax
from jax.experimental import pallas as pl
from jax.experimental.pallas import tpu as pltpu
from jax.sharding import PartitionSpec as P

EPS = 1e-06
MESH = pl.DeviceIdType.MESH
NY, NC, NZ = 4, 2, 16
NT = NY * NC
BLK = 16
F32, BF16 = jnp.float32, jnp.bfloat16
NEAR = 4
NEAR_SLOTS = 2 * NEAR + 1
GROUPS = [[(4, 1)], [(2, 2), (5, 2)], [(0, 2), (7, 2)], [(9, 7)]]
FAR_OFFSETS = [8, 7, 9, 6, 10, 5, 11]
NEAR_OFFSETS = [4, 12, 3, 13, 2, 14, 1, 15]
Z_ORDER = FAR_OFFSETS + NEAR_OFFSETS
Y_ORDER = [2, 1, 3]


def slot_of(offset):
    return (offset + NEAR) % NZ


def kernel(
    tok_ref, gain_ref, tgt_ref, u_hbm, loss_ref, grad_ref,
    xs, us, ug, logits, q, term, send_t, send_o, core_t, core_o, y_t, y_o, own, z_send, z_recv,
    stat_send, stat_y, group, stat_z, twice, twice_int, u_sem, send_sem, recv_sem,
):
    dp = lax.axis_index("dp")
    t = lax.axis_index("tensor")
    z = lax.axis_index("pipe")
    y, c = t // NC, t % NC
    rows = BLK * NZ
    near_rows = NEAR_SLOTS * BLK
    width = tok_ref.shape[1]
    lanes = width // 128
    vocab = us.shape[1]
    count = [0]
    started = []

    def tensor_of(dy, dc):
        return lax.rem(y + dy, NY) * NC + lax.rem(c + dc, NC)

    def at_tensor(dy, dc):
        return (dp, tensor_of(dy, dc), z)

    def at_pipe(d):
        return (dp, t, lax.rem(z + d, NZ))

    def send(src, dst, device):
        i = count[0]
        count[0] += 1
        copy = pltpu.make_async_remote_copy(
            src_ref=src, dst_ref=dst, send_sem=send_sem.at[i], recv_sem=recv_sem.at[i],
            device_id=device, device_id_type=MESH,
        )
        copy.start()
        started.append(copy)
        return copy

    def slots(first, number=1):
        return pl.ds(first * BLK, number * BLK)

    def gain_of(k):
        return jnp.concatenate([gain_ref[pl.ds(lanes * k + i, 1), :] for i in range(lanes)], axis=1)

    barrier = pltpu.get_barrier_semaphore()
    for d in range(1, NZ):
        pl.semaphore_signal(barrier, inc=1, device_id=at_pipe(d), device_id_type=MESH)
    for j in range(1, NT):
        pl.semaphore_signal(barrier, inc=1, device_id=at_tensor(j // NC, j % NC), device_id_type=MESH)

    loads = []
    for k in range(NT):
        load = pltpu.make_async_copy(u_hbm.at[:, pl.ds(k * width, width)], us.at[k], u_sem.at[k])
        load.start()
        loads.append(load)
    own_copy = pltpu.make_async_copy(tok_ref, xs.at[t, slots(NEAR)], u_sem.at[NT])
    own_copy.start()

    for h in range(2):
        part = jnp.transpose(jnp.broadcast_to(tgt_ref[h : h + 1, :], (128, 128)))
        twice_int[pl.ds(h * 128, 128), :] = part
        twice_int[pl.ds(rows + h * 128, 128), :] = part
    first_block = lax.rem(z + NZ - NEAR, NZ)
    shift = pl.multiple_of(first_block * BLK, BLK)
    back = pl.multiple_of(rows - first_block * BLK, BLK)
    vocab_start = (t * NZ + z) * vocab
    own_copy.wait()
    pl.semaphore_wait(barrier, NZ - 1 + NT - 1)

    z_copies = {}
    for d in NEAR_OFFSETS:
        z_copies[slot_of(NZ - d)] = send(tok_ref, xs.at[t, slots(slot_of(NZ - d))], at_pipe(d))
    y_copies, core_copies = [], [[], [], [], []]

    def forward(g):
        for first, number in GROUPS[g]:
            piece = xs.at[t, slots(first, number)]
            for dy in Y_ORDER:
                y_copies.append((g, dy, first, number, send(piece, piece, at_tensor(dy, 0))))
            core_copies[g].append(send(piece, piece, at_tensor(0, 1)))

    def hand_over(g):
        for group_of, dy, first, number, copy in y_copies:
            if group_of == g:
                copy.wait_recv()
                piece = xs.at[tensor_of(NY - dy, 0), slots(first, number)]
                core_copies[g].append(send(piece, piece, at_tensor(0, 1)))

    def wait_group(g):
        for first, number in GROUPS[g]:
            for s in range(first, first + number):
                if s != 0 and s != NEAR_SLOTS - 1:
                    z_copies[s].wait_recv()

    forward(0)
    for k in range(NT):
        loads[k].wait()
    lane = lax.broadcasted_iota(jnp.int32, (rows, vocab), 1)
    local = twice_int[pl.ds(shift, rows), :] - vocab_start
    local = jnp.concatenate([local] * ((vocab + 127) // 128), axis=1)[:, :vocab]
    q[...] = (lane == local).astype(F32).astype(BF16)
    o_core, o_y = {}, {}
    for dy in Y_ORDER:
        k = tensor_of(dy, 1)
        send_o[k] = jnp.dot(q[...], us[k], preferred_element_type=F32).astype(BF16)
        o_core[dy] = send(send_o.at[k], core_o.at[dy], at_tensor(0, 1))
    wait_group(1)
    forward(1)
    z_copies[0].wait_recv()
    z_copies[NEAR_SLOTS - 1].wait_recv()
    far_ahead = xs.at[t, slots(0)]
    far_behind = xs.at[t, slots(NEAR_SLOTS - 1)]
    across = xs.at[t, pl.ds(pl.multiple_of(c * ((NEAR_SLOTS - 1) * BLK), BLK), BLK)]
    z_copies[slot_of(8)] = send(across, xs.at[t, slots(slot_of(8))], at_pipe(NEAR + c * (NZ - 2 * NEAR)))
    for j in (3, 2, 1):
        z_copies[NZ - j] = send(far_ahead, xs.at[t, slots(NZ - j)], at_pipe(j))
        z_copies[NEAR_SLOTS - 1 + j] = send(far_behind, xs.at[t, slots(NEAR_SLOTS - 1 + j)], at_pipe(NZ - j))
    wait_group(2)
    forward(2)
    hand_over(0)
    for dy in (0,):
        k = tensor_of(dy, 1)
        send_o[k] = jnp.dot(q[...], us[k], preferred_element_type=F32).astype(BF16)
        o_core[dy] = send(send_o.at[k], core_o.at[dy], at_tensor(0, 1))

    def sum_target(dy):
        k = tensor_of(dy, 0)
        mine = jnp.dot(q[...], us[k], preferred_element_type=F32)
        o_core[dy].wait_recv()
        send_o[k] = (mine + core_o[dy].astype(F32)).astype(BF16)

    def send_target(dy):
        k = tensor_of(dy, 0)
        o_y[dy] = send(send_o.at[k], y_o.at[dy - 1], at_tensor(dy, 0))

    sum_target(Y_ORDER[0])
    send_target(Y_ORDER[0])
    hand_over(1)

    def scale_u(k, _):
        ug[k] = (us[k].astype(F32) * gain_of(k)).astype(BF16)
        return 0

    lax.fori_loop(0, NT, scale_u, 0)
    wait_group(3)
    forward(3)
    hand_over(2)

    def products(first, size):
        part = pl.ds(first, size)
        logits[part, :] = jnp.zeros((size, vocab), F32)

        def multiply(k, total):
            x = xs[k, part, :]
            logits[part, :] += lax.dot_general(x, ug[k], (((1,), (1,)), ((), ())), preferred_element_type=F32)
            xf = x.astype(F32)
            xf = xf * xf
            for i in range(lanes):
                total = total + xf[:, i * 128 : (i + 1) * 128]
            return total

        squares = lax.fori_loop(0, NT, multiply, jnp.zeros((size, 128), F32))
        return lax.rsqrt(jnp.sum(squares, axis=1, keepdims=True) / (width * NT) + EPS)

    def softmax(first, size, inv):
        lane_id = lax.broadcasted_iota(jnp.int32, (size, 128), 1)
        column = lax.broadcasted_iota(jnp.int32, (size, vocab), 1)
        part = pl.ds(first, size)
        l = logits[part, :] * inv
        tgt = twice_int[pl.ds(pl.multiple_of(shift + first, BLK), size), :][:, :1] - vocab_start
        here = column == tgt
        top = jnp.max(l, axis=1, keepdims=True)
        e = jnp.where(here, 0.0, jnp.exp(l - top))
        q[part, :] = e.astype(BF16)
        total = jnp.sum(e, axis=1, keepdims=True)
        mixed = jnp.sum(e * l, axis=1, keepdims=True)
        picked = jnp.sum(jnp.where(here, l, 0.0), axis=1, keepdims=True)
        stats = jnp.where(lane_id == 0, top, jnp.where(lane_id == 1, total, jnp.where(lane_id == 2, mixed, picked)))
        twice[part, :] = stats
        twice[pl.ds(rows + first, size), :] = stats

    for dy in Y_ORDER[1:] + [0]:
        sum_target(dy)
    for g in range(3):
        for copy in core_copies[g]:
            copy.wait_recv()
    inv = products(0, near_rows)
    own_inv = inv[NEAR * BLK : (NEAR + 1) * BLK]
    for first in range(0, near_rows, 48):
        softmax(first, 48, inv[first : first + 48])
    hand_over(3)
    for dy in Y_ORDER[1:]:
        send_target(dy)
    for copy in core_copies[3]:
        copy.wait_recv()
    inv = products(near_rows, rows - near_rows)
    softmax(near_rows, 64, inv[:64])
    softmax(near_rows + 64, 48, inv[64:])
    for h in range(2):
        start = pl.multiple_of(back if h == 0 else lax.rem(back + 128, rows), BLK)
        turned = jnp.transpose(twice[pl.ds(start, 128), :])
        for i in range(4):
            stat_send[pl.ds(2 * i + h, 1), :] = turned[i : i + 1, :]
    y_stats = []
    for j in range(1, NT):
        y_stats.append(send(stat_send, stat_y.at[j], at_tensor(j // NC, j % NC)))

    t_core, t_y = {}, {}
    for dy in Y_ORDER + [0]:
        k = tensor_of(dy, 1)
        send_t[k] = jnp.dot(q[...], us[k], preferred_element_type=F32).astype(BF16)
        t_core[dy] = send(send_t.at[k], core_t.at[dy], at_tensor(0, 1))
    for dy in Y_ORDER + [0]:
        term[dy] = jnp.dot(q[...], us[tensor_of(dy, 0)], preferred_element_type=F32)

    def merge(tiles):
        top = tiles[0][0:2]
        for tile in tiles[1:]:
            top = jnp.maximum(top, tile[0:2])
        total = mixed = picked = jnp.zeros((2, 128), F32)
        for tile in tiles:
            factor = jnp.exp(tile[0:2] - top)
            total = total + factor * tile[2:4]
            mixed = mixed + factor * tile[4:6]
            picked = picked + tile[6:8]
        return top, total, mixed, picked

    def spread(value):
        for h in range(2):
            part = jnp.transpose(jnp.broadcast_to(value[h : h + 1, :], (128, 128)))
            twice[pl.ds(h * 128, 128), :] = part
            twice[pl.ds(rows + h * 128, 128), :] = part
        return twice[pl.ds(shift, rows), :]

    for copy in y_stats:
        copy.wait_recv()
    mine = stat_send[...]
    top, total, mixed, picked = merge([mine] + [stat_y[j] for j in range(1, NT)])
    group[0:2, :] = top
    group[2:4, :] = total
    group[4:6, :] = mixed
    group[6:8, :] = picked
    z_stats = []
    for d in Z_ORDER:
        z_stats.append(send(group, stat_z.at[d], at_pipe(d)))
    own[0] = spread(jnp.exp(mine[0:2] - top))
    own[1] = spread(jnp.exp(stat_y[1][0:2] - top))
    far, near = (near_rows, rows - near_rows), (0, near_rows)

    def add_core(dy, first, size):
        part = pl.ds(first, size)
        own_factor = jnp.concatenate([own[0, part, :]] * lanes, axis=1)
        core_factor = jnp.concatenate([own[1, part, :]] * lanes, axis=1)
        return term[dy, part, :] * own_factor + core_t[dy, part, :].astype(F32) * core_factor

    for first, size in (far, near):
        part = pl.ds(first, size)
        for dy in Y_ORDER:
            if first:
                t_core[dy].wait_recv()
            k = tensor_of(dy, 0)
            send_t[k, part, :] = add_core(dy, first, size).astype(BF16)
            t_y[dy, first] = send(send_t.at[k, part], y_t.at[dy - 1, part], at_tensor(dy, 0))
    t_core[0].wait_recv()
    for dy in Y_ORDER:
        o_y[dy].wait_recv()
    for first, size in (far, near):
        part = pl.ds(first, size)
        target = send_o[t, part, :].astype(F32)
        for dy in range(NY - 1):
            target = target + y_o[dy, part, :].astype(F32)
        term[1, part, :] = target
        term[0, part, :] = add_core(0, first, size)
    for copy in z_stats:
        copy.wait_recv()
    group_top = group[0:2]
    top, total, mixed, picked = merge([group[...]] + [stat_z[d] for d in range(1, NZ)])
    full = total + jnp.exp(picked - top)
    loss_ref[...] = top + jnp.log(full) - picked
    own[0] = spread(jnp.exp(group_top - top) / full)
    own[1] = spread(total / full)
    own_dot = spread((mixed - total * picked) / full)[NEAR * BLK : (NEAR + 1) * BLK]
    z_grads = {}
    for (first, size), offsets in ((far, FAR_OFFSETS), (near, NEAR_OFFSETS)):
        part = pl.ds(first, size)
        for dy in Y_ORDER:
            t_y[dy, first].wait_recv()
        value = term[0, part, :]
        for dy in range(NY - 1):
            value = value + y_t[dy, part, :].astype(F32)
        scale = jnp.concatenate([own[0, part, :]] * lanes, axis=1)
        drop = jnp.concatenate([own[1, part, :]] * lanes, axis=1)
        value = value * scale - term[1, part, :] * drop
        z_send[part, :] = value.astype(BF16)
        if first == 0:
            term[2, slots(NEAR), :] = value[NEAR * BLK : (NEAR + 1) * BLK]
        for d in offsets:
            z_grads[d] = send(z_send.at[slots(slot_of(d))], z_recv.at[d], at_pipe(d))
    grad = term[2, slots(NEAR), :]
    for d in reversed(Z_ORDER):
        z_grads[d].wait_recv()
        grad = grad + z_recv[d].astype(F32)
    stream = tok_ref[...].astype(F32)
    weighted = grad * gain_of(t)
    dots = own_dot[:, :1] / (own_inv * (width * NT))
    grad_ref[...] = own_inv * (weighted - stream * (own_inv * own_inv * dots))
    for copy in started:
        copy.wait_send()


def body(tokens, final_gain, unembed, targets):
    vocab, features = unembed.shape
    width = tokens.shape[1]
    rows = targets.shape[0]
    vmem = pl.BlockSpec(memory_space=pltpu.VMEM)
    loss, grad = pl.pallas_call(
        kernel,
        out_shape=(
            jax.ShapeDtypeStruct((2, 128), F32),
            jax.ShapeDtypeStruct(tokens.shape, F32),
        ),
        in_specs=[vmem, vmem, vmem, pl.BlockSpec(memory_space=pl.ANY)],
        out_specs=(vmem, vmem),
        scratch_shapes=[
            pltpu.VMEM((NT, rows, width), BF16),
            pltpu.VMEM((NT, vocab, width), BF16),
            pltpu.VMEM((NT, vocab, width), BF16),
            pltpu.VMEM((rows, vocab), F32),
            pltpu.VMEM((rows, vocab), BF16),
            pltpu.VMEM((NY, rows, width), F32),
            pltpu.VMEM((NT, rows, width), BF16),
            pltpu.VMEM((NT, rows, width), BF16),
            pltpu.VMEM((NY, rows, width), BF16),
            pltpu.VMEM((NY, rows, width), BF16),
            pltpu.VMEM((NY - 1, rows, width), BF16),
            pltpu.VMEM((NY - 1, rows, width), BF16),
            pltpu.VMEM((2, rows, 128), F32),
            pltpu.VMEM((rows, width), BF16),
            pltpu.VMEM((NZ, BLK, width), BF16),
            pltpu.VMEM((8, 128), F32),
            pltpu.VMEM((NT, 8, 128), F32),
            pltpu.VMEM((8, 128), F32),
            pltpu.VMEM((NZ, 8, 128), F32),
            pltpu.VMEM((2 * rows, 128), F32),
            pltpu.VMEM((2 * rows, 128), jnp.int32),
            pltpu.SemaphoreType.DMA((NT + 1,)),
            pltpu.SemaphoreType.DMA((160,)),
            pltpu.SemaphoreType.DMA((160,)),
        ],
        compiler_params=pltpu.CompilerParams(
            collective_id=0, has_side_effects=True, vmem_limit_bytes=60 * 1024 * 1024
        ),
    )(tokens, final_gain.reshape(features // 128, 128), targets.reshape(2, 128), unembed)
    return loss.reshape(rows), grad


def solution(mesh):
    placed = (P(("dp", "pipe"), "tensor"), P(), P(("tensor", "pipe"), None), P("dp"))
    return jax.shard_map(
        body,
        mesh=mesh,
        in_specs=placed,
        out_specs=(P("dp"), P(("dp", "pipe"), "tensor")),
        check_vma=False,
    )
```

time: 92.1 us -> 78.7 us (0.85)
  Pallas kernels: 87.2 us -> 75.2 us
  local copies, waits for them, and re-layouts: 3.93 us -> 2.6 us
    pallas_call x1, Pallas kernels: 87.2 us -> 75.2 us  [body(): pl.pallas_call(kernel, out_shape=(jax.ShapeDtypeStruct((2, 128), F32), ja...]
    reshape x1 -> x0, local copies, waits for them, and re-layouts: 1.33 us -> none  [body(): final_gain.reshape(NT, width)]
where the time goes in v2:
time: 78.7 us; the launch traced here: 78.5 us
  Pallas kernels  75.2 us (96%)
  local copies, waits for them, and re-layouts  2.6 us (3%)
    pallas_call x1, Pallas kernels, body(): pl.pallas_call(kernel, out_shape=(jax.ShapeDtypeStruct((2, 128), F32), ja...  75.2 us
    unnamed x2, local copies, waits for them, and re-layouts  2.6 us

profile of v2, /device:TPU:1, one launch (start us, length us, event | category | flops | bytes accessed | tf_op | source)
XLA Modules:
  0.0 78.5 jit_solution(10594248654714856060)
XLA Ops:
  0.6 75.2 %shard_map.59 = (f32[2,128]{1,0:T(2,128)}, f32[16,512]{1,0:T(8,128)}) custom-call(bf16[16,512]{1,0:T(8,128)(2,1)} %tok_ref.1, f32[32,128]{1,0:T(8,128)} %bitcast.3, s32[2,128]{1,0:T(2,128)} %bitcast.5, bf16[600,4096]{1,0:T(8,128)(2,1)} %u_hbm.1), custom_call_target="tpu_custom_call" | custom-call | tf_op jit(solution)/shard_map/pallas_call | solution.py:343
  75.9 1.2 %copy.8 = f32[256]{0:T(256)} copy(f32[256]{0:T(256)} %bitcast.4) | data formatting | bytes 2048
  77.1 1.4 %copy.9 = f32[16,512]{1,0:T(8,128)} copy(f32[16,512]{1,0:T(8,128)} %get-tuple-element.9) | data formatting | bytes 65536

commit v3 on v2

--- a/solution.py
+++ b/solution.py
@@ -15,11 +15,12 @@
 F32, BF16 = jnp.float32, jnp.bfloat16
 NEAR = 4
 NEAR_SLOTS = 2 * NEAR + 1
-GROUPS = [[(4, 1)], [(2, 2), (5, 2)], [(0, 2), (7, 2)], [(9, 7)]]
+GROUPS = [[(4, 1)], [(2, 2), (5, 2)], [(0, 2), (7, 2)], [(9, 2), (14, 2)], [(11, 3)]]
 FAR_OFFSETS = [8, 7, 9, 6, 10, 5, 11]
 NEAR_OFFSETS = [4, 12, 3, 13, 2, 14, 1, 15]
 Z_ORDER = FAR_OFFSETS + NEAR_OFFSETS
 Y_ORDER = [2, 1, 3]
+SUMS = [([(9, 7)], FAR_OFFSETS), ([(0, 3), (6, 3)], NEAR_OFFSETS[:6]), ([(3, 3)], NEAR_OFFSETS[6:])]
 
 
 def slot_of(offset):
@@ -97,7 +98,7 @@
     z_copies = {}
     for d in NEAR_OFFSETS:
         z_copies[slot_of(NZ - d)] = send(tok_ref, xs.at[t, slots(slot_of(NZ - d))], at_pipe(d))
-    y_copies, core_copies = [], [[], [], [], []]
+    y_copies, core_copies = [], [[] for _ in GROUPS]
 
     def forward(g):
         for first, number in GROUPS[g]:
@@ -139,7 +140,7 @@
     far_behind = xs.at[t, slots(NEAR_SLOTS - 1)]
     across = xs.at[t, pl.ds(pl.multiple_of(c * ((NEAR_SLOTS - 1) * BLK), BLK), BLK)]
     z_copies[slot_of(8)] = send(across, xs.at[t, slots(slot_of(8))], at_pipe(NEAR + c * (NZ - 2 * NEAR)))
-    for j in (3, 2, 1):
+    for j in (1, 2, 3):
         z_copies[NZ - j] = send(far_ahead, xs.at[t, slots(NZ - j)], at_pipe(j))
         z_copies[NEAR_SLOTS - 1 + j] = send(far_behind, xs.at[t, slots(NEAR_SLOTS - 1 + j)], at_pipe(NZ - j))
     wait_group(2)
@@ -171,6 +172,8 @@
     lax.fori_loop(0, NT, scale_u, 0)
     wait_group(3)
     forward(3)
+    wait_group(4)
+    forward(4)
     hand_over(2)
 
     def products(first, size):
@@ -216,9 +219,10 @@
     for first in range(0, near_rows, 48):
         softmax(first, 48, inv[first : first + 48])
     hand_over(3)
+    hand_over(4)
     for dy in Y_ORDER[1:]:
         send_target(dy)
-    for copy in core_copies[3]:
+    for copy in core_copies[3] + core_copies[4]:
         copy.wait_recv()
     inv = products(near_rows, rows - near_rows)
     softmax(near_rows, 64, inv[:64])
@@ -267,37 +271,38 @@
     group[2:4, :] = total
     group[4:6, :] = mixed
     group[6:8, :] = picked
-    z_stats = []
-    for d in Z_ORDER:
-        z_stats.append(send(group, stat_z.at[d], at_pipe(d)))
     own[0] = spread(jnp.exp(mine[0:2] - top))
     own[1] = spread(jnp.exp(stat_y[1][0:2] - top))
-    far, near = (near_rows, rows - near_rows), (0, near_rows)
-
-    def add_core(dy, first, size):
-        part = pl.ds(first, size)
+
+    def add_core(dy, part):
         own_factor = jnp.concatenate([own[0, part, :]] * lanes, axis=1)
         core_factor = jnp.concatenate([own[1, part, :]] * lanes, axis=1)
         return term[dy, part, :] * own_factor + core_t[dy, part, :].astype(F32) * core_factor
 
-    for first, size in (far, near):
-        part = pl.ds(first, size)
+    z_stats = []
+    for pieces, _ in SUMS:
         for dy in Y_ORDER:
-            if first:
+            if not z_stats:
                 t_core[dy].wait_recv()
             k = tensor_of(dy, 0)
-            send_t[k, part, :] = add_core(dy, first, size).astype(BF16)
-            t_y[dy, first] = send(send_t.at[k, part], y_t.at[dy - 1, part], at_tensor(dy, 0))
+            for first, number in pieces:
+                part = slots(first, number)
+                send_t[k, part, :] = add_core(dy, part).astype(BF16)
+                t_y[dy, first] = send(send_t.at[k, part], y_t.at[dy - 1, part], at_tensor(dy, 0))
+        if not z_stats:
+            for d in Z_ORDER:
+                z_stats.append(send(group, stat_z.at[d], at_pipe(d)))
     t_core[0].wait_recv()
     for dy in Y_ORDER:
         o_y[dy].wait_recv()
-    for first, size in (far, near):
-        part = pl.ds(first, size)
-        target = send_o[t, part, :].astype(F32)
-        for dy in range(NY - 1):
-            target = target + y_o[dy, part, :].astype(F32)
-        term[1, part, :] = target
-        term[0, part, :] = add_core(0, first, size)
+    for pieces, _ in SUMS:
+        for first, number in pieces:
+            part = slots(first, number)
+            target = send_o[t, part, :].astype(F32)
+            for dy in range(NY - 1):
+                target = target + y_o[dy, part, :].astype(F32)
+            term[1, part, :] = target
+            term[0, part, :] = add_core(0, part)
     for copy in z_stats:
         copy.wait_recv()
     group_top = group[0:2]
@@ -308,23 +313,24 @@
     own[1] = spread(total / full)
     own_dot = spread((mixed - total * picked) / full)[NEAR * BLK : (NEAR + 1) * BLK]
     z_grads = {}
-    for (first, size), offsets in ((far, FAR_OFFSETS), (near, NEAR_OFFSETS)):
-        part = pl.ds(first, size)
-        for dy in Y_ORDER:
-            t_y[dy, first].wait_recv()
-        value = term[0, part, :]
-        for dy in range(NY - 1):
-            value = value + y_t[dy, part, :].astype(F32)
-        scale = jnp.concatenate([own[0, part, :]] * lanes, axis=1)
-        drop = jnp.concatenate([own[1, part, :]] * lanes, axis=1)
-        value = value * scale - term[1, part, :] * drop
-        z_send[part, :] = value.astype(BF16)
-        if first == 0:
-            term[2, slots(NEAR), :] = value[NEAR * BLK : (NEAR + 1) * BLK]
+    for pieces, offsets in SUMS:
+        for first, number in pieces:
+            part = slots(first, number)
+            for dy in Y_ORDER:
+                t_y[dy, first].wait_recv()
+            value = term[0, part, :]
+            for dy in range(NY - 1):
+                value = value + y_t[dy, part, :].astype(F32)
+            scale = jnp.concatenate([own[0, part, :]] * lanes, axis=1)
+            drop = jnp.concatenate([own[1, part, :]] * lanes, axis=1)
+            value = value * scale - term[1, part, :] * drop
+            z_send[part, :] = value.astype(BF16)
+            if first <= NEAR < first + number:
+                term[2, slots(NEAR), :] = value[(NEAR - first) * BLK : (NEAR - first + 1) * BLK]
         for d in offsets:
             z_grads[d] = send(z_send.at[slots(slot_of(d))], z_recv.at[d], at_pipe(d))
     grad = term[2, slots(NEAR), :]
-    for d in reversed(Z_ORDER):
+    for d in Z_ORDER:
         z_grads[d].wait_recv()
         grad = grad + z_recv[d].astype(F32)
     stream = tok_ref[...].astype(F32)
@@ -335,17 +341,23 @@
         copy.wait_send()
 
 
+def hand_out(loss_ref, grad_ref, loss_out, grad_out):
+    loss_out[...] = loss_ref[...]
+    grad_out[...] = grad_ref[...]
+
+
 def body(tokens, final_gain, unembed, targets):
     vocab, features = unembed.shape
     width = tokens.shape[1]
     rows = targets.shape[0]
     vmem = pl.BlockSpec(memory_space=pltpu.VMEM)
+    results = (
+        jax.ShapeDtypeStruct((2, 128), F32),
+        jax.ShapeDtypeStruct(tokens.shape, F32),
+    )
     loss, grad = pl.pallas_call(
         kernel,
-        out_shape=(
-            jax.ShapeDtypeStruct((2, 128), F32),
-            jax.ShapeDtypeStruct(tokens.shape, F32),
-        ),
+        out_shape=results,
         in_specs=[vmem, vmem, vmem, pl.BlockSpec(memory_space=pl.ANY)],
         out_specs=(vmem, vmem),
         scratch_shapes=[
@@ -378,6 +390,9 @@
             collective_id=0, has_side_effects=True, vmem_limit_bytes=60 * 1024 * 1024
         ),
     )(tokens, final_gain.reshape(features // 128, 128), targets.reshape(2, 128), unembed)
+    loss, grad = pl.pallas_call(
+        hand_out, out_shape=results, in_specs=[vmem, vmem], out_specs=(vmem, vmem)
+    )(loss, grad)
     return loss.reshape(rows), grad
 
 

time: 78.7 us -> 75.8 us (0.963)
  local copies, waits for them, and re-layouts: 2.6 us -> 0 us
    unnamed x2 -> x0, local copies, waits for them, and re-layouts: 2.6 us -> none
    pallas_call x1 -> x2, Pallas kernels: 75.2 us -> 75 us  [the longest x1 73.6 us: body(): pl.pallas_call(kernel, out_shape=results, in_specs=[vmem, vmem, vmem, pl....]
where the time goes in v3:
time: 75.8 us; the launch traced here: 75.6 us
  Pallas kernels  75 us (99%)
    pallas_call x1, Pallas kernels, body(): pl.pallas_call(kernel, out_shape=results, in_specs=[vmem, vmem, vmem, pl....  73.6 us

profile of v3, /device:TPU:1, one launch (start us, length us, event | category | flops | bytes accessed | tf_op | source)
XLA Modules:
  0.0 75.6 jit_solution(13881326558391187617)
XLA Ops:
  0.6 73.6 %shard_map.59 = (f32[2,128]{1,0:T(2,128)}, f32[16,512]{1,0:T(8,128)}) custom-call(bf16[16,512]{1,0:T(8,128)(2,1)} %tok_ref.1, f32[32,128]{1,0:T(8,128)} %bitcast.3, s32[2,128]{1,0:T(2,128)} %bitcast.4, bf16[600,4096]{1,0:T(8,128)(2,1)} %u_hbm.1), custom_call_target="tpu_custom_call" | custom-call | tf_op jit(solution)/shard_map/pallas_call | solution.py:358
  74.2 1.4 %shard_map.60 = (f32[2,128]{1,0:T(2,128)}, f32[16,512]{1,0:T(8,128)}) custom-call(f32[2,128]{1,0:T(2,128)} %get-tuple-element.6.loss_ref, f32[16,512]{1,0:T(8,128)} %get-tuple-element.7.grad_ref), custom_call_target="tpu_custom_call" | custom-call | tf_op jit(solution)/shard_map/pallas_call | solution.py:393

commit v4 on v3

--- a/solution.py
+++ b/solution.py
@@ -20,7 +20,7 @@
 NEAR_OFFSETS = [4, 12, 3, 13, 2, 14, 1, 15]
 Z_ORDER = FAR_OFFSETS + NEAR_OFFSETS
 Y_ORDER = [2, 1, 3]
-SUMS = [([(9, 7)], FAR_OFFSETS), ([(0, 3), (6, 3)], NEAR_OFFSETS[:6]), ([(3, 3)], NEAR_OFFSETS[6:])]
+SUMS = [([(11, 3)], FAR_OFFSETS[:3]), ([(9, 2), (14, 2)], FAR_OFFSETS[3:]), ([(0, 3), (6, 3)], NEAR_OFFSETS[:6]), ([(3, 3)], NEAR_OFFSETS[6:])]
 
 
 def slot_of(offset):
@@ -29,7 +29,7 @@
 
 def kernel(
     tok_ref, gain_ref, tgt_ref, u_hbm, loss_ref, grad_ref,
-    xs, us, ug, logits, q, term, send_t, send_o, core_t, core_o, y_t, y_o, own, z_send, z_recv,
+    xs, us, ug, logits, q, term, send_t, send_o, core_t, core_o, y_t, y_o, o_half, own, z_send, z_recv,
     stat_send, stat_y, group, stat_z, twice, twice_int, u_sem, send_sem, recv_sem,
 ):
     dp = lax.axis_index("dp")
@@ -151,18 +151,26 @@
         send_o[k] = jnp.dot(q[...], us[k], preferred_element_type=F32).astype(BF16)
         o_core[dy] = send(send_o.at[k], core_o.at[dy], at_tensor(0, 1))
 
+    half = width // 2
+    cuts = {1: pl.ds(0, half), 3: pl.ds(half, half)}
+    o_through = {}
+
     def sum_target(dy):
         k = tensor_of(dy, 0)
-        mine = jnp.dot(q[...], us[k], preferred_element_type=F32)
+        total = jnp.dot(q[...], us[k], preferred_element_type=F32)
         o_core[dy].wait_recv()
-        send_o[k] = (mine + core_o[dy].astype(F32)).astype(BF16)
+        send_o[k] = (total + core_o[dy].astype(F32)).astype(BF16)
+        if dy in cuts:
+            o_through[dy].wait_recv()
+            passing = o_half[dy // 2].astype(F32)
+            send_o[k, :, cuts[dy]] = (send_o[k, :, cuts[dy]].astype(F32) + passing).astype(BF16)
 
     def send_target(dy):
-        k = tensor_of(dy, 0)
-        o_y[dy] = send(send_o.at[k], y_o.at[dy - 1], at_tensor(dy, 0))
-
-    sum_target(Y_ORDER[0])
-    send_target(Y_ORDER[0])
+        o_y[dy] = send(send_o.at[tensor_of(dy, 0)], y_o.at[dy // 2], at_tensor(dy, 0))
+
+    sum_target(2)
+    for dy in cuts:
+        o_through[dy] = send(send_o.at[tensor_of(2, 0), :, cuts[dy]], o_half.at[dy // 2], at_tensor(dy, 0))
     hand_over(1)
 
     def scale_u(k, _):
@@ -220,7 +228,7 @@
         softmax(first, 48, inv[first : first + 48])
     hand_over(3)
     hand_over(4)
-    for dy in Y_ORDER[1:]:
+    for dy in cuts:
         send_target(dy)
     for copy in core_copies[3] + core_copies[4]:
         copy.wait_recv()
@@ -271,6 +279,9 @@
     group[2:4, :] = total
     group[4:6, :] = mixed
     group[6:8, :] = picked
+    z_stats = []
+    for d in Z_ORDER:
+        z_stats.append(send(group, stat_z.at[d], at_pipe(d)))
     own[0] = spread(jnp.exp(mine[0:2] - top))
     own[1] = spread(jnp.exp(stat_y[1][0:2] - top))
 
@@ -279,28 +290,24 @@
         core_factor = jnp.concatenate([own[1, part, :]] * lanes, axis=1)
         return term[dy, part, :] * own_factor + core_t[dy, part, :].astype(F32) * core_factor
 
-    z_stats = []
     for pieces, _ in SUMS:
         for dy in Y_ORDER:
-            if not z_stats:
+            if pieces[0][0] == SUMS[0][0][0][0]:
                 t_core[dy].wait_recv()
             k = tensor_of(dy, 0)
             for first, number in pieces:
                 part = slots(first, number)
                 send_t[k, part, :] = add_core(dy, part).astype(BF16)
                 t_y[dy, first] = send(send_t.at[k, part], y_t.at[dy - 1, part], at_tensor(dy, 0))
-        if not z_stats:
-            for d in Z_ORDER:
-                z_stats.append(send(group, stat_z.at[d], at_pipe(d)))
     t_core[0].wait_recv()
-    for dy in Y_ORDER:
+    for dy in cuts:
         o_y[dy].wait_recv()
     for pieces, _ in SUMS:
         for first, number in pieces:
             part = slots(first, number)
             target = send_o[t, part, :].astype(F32)
-            for dy in range(NY - 1):
-                target = target + y_o[dy, part, :].astype(F32)
+            for i in range(2):
+                target = target + y_o[i, part, :].astype(F32)
             term[1, part, :] = target
             term[0, part, :] = add_core(0, part)
     for copy in z_stats:
@@ -372,7 +379,8 @@
             pltpu.VMEM((NY, rows, width), BF16),
             pltpu.VMEM((NY, rows, width), BF16),
             pltpu.VMEM((NY - 1, rows, width), BF16),
-            pltpu.VMEM((NY - 1, rows, width), BF16),
+            pltpu.VMEM((2, rows, width), BF16),
+            pltpu.VMEM((2, rows, width // 2), BF16),
             pltpu.VMEM((2, rows, 128), F32),
             pltpu.VMEM((rows, width), BF16),
             pltpu.VMEM((NZ, BLK, width), BF16),

time: 75.8 us -> 72.2 us (0.953)
  Pallas kernels: 75 us -> 71.2 us
    pallas_call x1, Pallas kernels: 73.6 us -> 69.9 us  [body(): pl.pallas_call(kernel, out_shape=results, in_specs=[vmem, vmem, vmem, pl....]
where the time goes in v4:
time: 72.2 us; the launch traced here: 71.9 us
  Pallas kernels  71.2 us (99%)
    pallas_call x1, Pallas kernels, body(): pl.pallas_call(kernel, out_shape=results, in_specs=[vmem, vmem, vmem, pl....  69.9 us

profile of v4, /device:TPU:1, one launch (start us, length us, event | category | flops | bytes accessed | tf_op | source)
XLA Modules:
  0.0 71.9 jit_solution(6633657136274554381)
XLA Ops:
  0.6 69.9 %shard_map.59 = (f32[2,128]{1,0:T(2,128)}, f32[16,512]{1,0:T(8,128)}) custom-call(bf16[16,512]{1,0:T(8,128)(2,1)} %tok_ref.1, f32[32,128]{1,0:T(8,128)} %bitcast.3, s32[2,128]{1,0:T(2,128)} %bitcast.4, bf16[600,4096]{1,0:T(8,128)(2,1)} %u_hbm.1), custom_call_target="tpu_custom_call" | custom-call | tf_op jit(solution)/shard_map/pallas_call | solution.py:365
  70.5 1.4 %shard_map.60 = (f32[2,128]{1,0:T(2,128)}, f32[16,512]{1,0:T(8,128)}) custom-call(f32[2,128]{1,0:T(2,128)} %get-tuple-element.6.loss_ref, f32[16,512]{1,0:T(8,128)} %get-tuple-element.7.grad_ref), custom_call_target="tpu_custom_call" | custom-call | tf_op jit(solution)/shard_map/pallas_call | solution.py:401

commit v5 on v4

--- a/solution.py
+++ b/solution.py
@@ -29,7 +29,7 @@
 
 def kernel(
     tok_ref, gain_ref, tgt_ref, u_hbm, loss_ref, grad_ref,
-    xs, us, ug, logits, q, term, send_t, send_o, core_t, core_o, y_t, y_o, o_half, own, z_send, z_recv,
+    xs, us, ug, logits, q, term, send_t, send_o, core_t, core_o, y_t, y_o, o_half, t_half, own, z_send, z_recv,
     stat_send, stat_y, group, stat_z, twice, twice_int, u_sem, send_sem, recv_sem,
 ):
     dp = lax.axis_index("dp")
@@ -290,15 +290,30 @@
         core_factor = jnp.concatenate([own[1, part, :]] * lanes, axis=1)
         return term[dy, part, :] * own_factor + core_t[dy, part, :].astype(F32) * core_factor
 
+    t_through = {}
+    t_core[2].wait_recv()
     for pieces, _ in SUMS:
-        for dy in Y_ORDER:
-            if pieces[0][0] == SUMS[0][0][0][0]:
-                t_core[dy].wait_recv()
-            k = tensor_of(dy, 0)
-            for first, number in pieces:
+        for first, number in pieces:
+            part = slots(first, number)
+            send_t[tensor_of(2, 0), part, :] = add_core(2, part).astype(BF16)
+            for dy in cuts:
+                t_through[dy, first] = send(
+                    send_t.at[tensor_of(2, 0), part, cuts[dy]], t_half.at[dy // 2, part], at_tensor(dy, 0)
+                )
+    for dy in cuts:
+        t_core[dy].wait_recv()
+    for pieces, _ in SUMS:
+        for first, number in pieces:
+            for dy in cuts:
+                k = tensor_of(dy, 0)
                 part = slots(first, number)
-                send_t[k, part, :] = add_core(dy, part).astype(BF16)
-                t_y[dy, first] = send(send_t.at[k, part], y_t.at[dy - 1, part], at_tensor(dy, 0))
+                value = add_core(dy, part)
+                t_through[dy, first].wait_recv()
+                passing = t_half[dy // 2, part, :].astype(F32)
+                beside = jnp.zeros_like(passing)
+                passing = jnp.concatenate([passing, beside] if dy == 1 else [beside, passing], axis=1)
+                send_t[k, part, :] = (value + passing).astype(BF16)
+                t_y[dy, first] = send(send_t.at[k, part], y_t.at[dy // 2, part], at_tensor(dy, 0))
     t_core[0].wait_recv()
     for dy in cuts:
         o_y[dy].wait_recv()
@@ -323,11 +338,11 @@
     for pieces, offsets in SUMS:
         for first, number in pieces:
             part = slots(first, number)
-            for dy in Y_ORDER:
+            for dy in cuts:
                 t_y[dy, first].wait_recv()
             value = term[0, part, :]
-            for dy in range(NY - 1):
-                value = value + y_t[dy, part, :].astype(F32)
+            for i in range(2):
+                value = value + y_t[i, part, :].astype(F32)
             scale = jnp.concatenate([own[0, part, :]] * lanes, axis=1)
             drop = jnp.concatenate([own[1, part, :]] * lanes, axis=1)
             value = value * scale - term[1, part, :] * drop
@@ -378,8 +393,9 @@
             pltpu.VMEM((NT, rows, width), BF16),
             pltpu.VMEM((NY, rows, width), BF16),
             pltpu.VMEM((NY, rows, width), BF16),
-            pltpu.VMEM((NY - 1, rows, width), BF16),
             pltpu.VMEM((2, rows, width), BF16),
+            pltpu.VMEM((2, rows, width), BF16),
+            pltpu.VMEM((2, rows, width // 2), BF16),
             pltpu.VMEM((2, rows, width // 2), BF16),
             pltpu.VMEM((2, rows, 128), F32),
             pltpu.VMEM((rows, width), BF16),

time: 72.2 us -> 72.4 us (level)
  no operation moved by 1% of the time
where the time goes in v5:
time: 72.4 us; the launch traced here: 71.6 us
  Pallas kernels  71 us (98%)
    pallas_call x1, Pallas kernels, body(): pl.pallas_call(kernel, out_shape=results, in_specs=[vmem, vmem, vmem, pl....  69.6 us

profile of v5, /device:TPU:1, one launch (start us, length us, event | category | flops | bytes accessed | tf_op | source)
XLA Modules:
  0.0 71.6 jit_solution(16086367657845625902)
XLA Ops:
  0.6 69.6 %shard_map.59 = (f32[2,128]{1,0:T(2,128)}, f32[16,512]{1,0:T(8,128)}) custom-call(bf16[16,512]{1,0:T(8,128)(2,1)} %tok_ref.1, f32[32,128]{1,0:T(8,128)} %bitcast.3, s32[2,128]{1,0:T(2,128)} %bitcast.4, bf16[600,4096]{1,0:T(8,128)(2,1)} %u_hbm.1), custom_call_target="tpu_custom_call" | custom-call | tf_op jit(solution)/shard_map/pallas_call | solution.py:380
  70.3 1.4 %shard_map.60 = (f32[2,128]{1,0:T(2,128)}, f32[16,512]{1,0:T(8,128)}) custom-call(f32[2,128]{1,0:T(2,128)} %get-tuple-element.6.loss_ref, f32[16,512]{1,0:T(8,128)} %get-tuple-element.7.grad_ref), custom_call_target="tpu_custom_call" | custom-call | tf_op jit(solution)/shard_map/pallas_call | solution.py:417
